TPU v7x, 32 devices: a whole 2x2x4 slice. The times are simulated.
32 devices in a mesh: dp: 4 (over z), ctx: 8 (over y, x, core).
Axes of the slice: x: 2, y: 2, z: 4, core: 2. Of those that a mesh axis runs over, the one named last changes fastest.
Arguments:
- inputs: bfloat16 [4, 1024, 1408], P('dp', 'ctx'), may hold values from -8 to 8
- cotangent: bfloat16 [4, 1024, 1408], P('dp', 'ctx'), may hold values from -6 to 6
- keep_mask: int32 [4], P('dp'), may hold values 0 or 1
- ln_gain: float32 [1408], replicated, may hold values from 0.1 to 1.9
- ln_bias: float32 [1408], replicated, may hold values from -4 to 4
- w_qkv: bfloat16 [1408, 4224], replicated, may hold values from -2 to 2
- qv_bias: float32 [2, 1408], replicated, may hold values from -6 to 6
- w_proj: bfloat16 [1408, 1408], replicated, may hold values from -0.15625 to 0.15625
- proj_bias: float32 [1408], replicated, may hold values from -4 to 4
Outputs:
- block_out: bfloat16 [4, 1024, 1408], P('dp', 'ctx')
- grad_inputs: bfloat16 [4, 1024, 1408], P('dp', 'ctx')
- grad_w_qkv: float32 [1408, 3, 1408], P('dp', None, 'ctx')
- grad_w_proj: float32 [1408, 1408], P('ctx', 'dp')
- grad_ln_gain: float32 [1408], P(('dp', 'ctx'))
- grad_ln_bias: float32 [1408], P(('dp', 'ctx'))
- grad_qv_bias: float32 [2, 1408], P(None, ('dp', 'ctx'))
- grad_proj_bias: float32 [1408], P(('dp', 'ctx'))
All inputs are finite; a program needn't handle non-finite values. No bound on the sum of `keep_mask` on one device may be relied on, other than what follows from the above.
Results may differ from a plain program's by a relative error of at most 0.018.
The roundings to bfloat16 on the way count: a program that leaves them out, or rounds other values in their place, can miss the bound.
Values may be sent and summed in bfloat16 or wider, within the bound.
A program may use at most 128 MiB of HBM per device.

v0:
```python
import functools
import math

import jax
import jax.numpy as jnp
from jax import lax
from jax.experimental import pallas as pl
from jax.experimental.pallas import tpu as pltpu
from jax.sharding import PartitionSpec as P

HEADS = 16
PAD = 96
eps = 1e-06
keep_rate = 0.75
MESH = pl.DeviceIdType.MESH
f32 = jnp.float32
bf16 = jnp.bfloat16


def nt(left, right):
    return lax.dot_general(left, right, (((1,), (1,)), ((), ())), preferred_element_type=f32)


def nn(left, right):
    return jnp.dot(left, right, preferred_element_type=f32)


def turned(block):
    wide = block.astype(f32)
    fill = jnp.zeros((128 - PAD, wide.shape[1]), f32)
    return jnp.transpose(jnp.concatenate([wide, fill], axis=0))


def normalize(values):
    average = jnp.mean(values, axis=-1, keepdims=True)
    centred = values - average
    variance = jnp.mean(centred * centred, axis=-1, keepdims=True)
    inv_scale = lax.rsqrt(variance + eps)
    return centred * inv_scale, inv_scale


def kernel(
    n, ndp, hh, hw, grad_scale,
    survive_ref, x_ref, cot_ref, gain_ref, bias_ref, bqkv_ref, pbias_ref,
    wt_hbm, wp_hbm, wqkv_hbm, wproj_hbm,
    out_ref, gin_ref, gqk_ref, gvp_ref, small_ref,
    wt, wp, wqkv, wproj, lin, gb, qkv, tok, probs, att, ga, gan, dkv, gt,
    att_in, gt_in, gp, glt, rs_send, rs_recv, vec, vec_in, sums, sums_in,
    load_sem, ag_send, ag_recv, att_send, att_recv, gt_send, gt_recv,
    rs_ssem, rs_rsem, vs, vr, ss, sr, own_sem,
):
    tokens, width = x_ref.shape
    length = tokens * n
    me = lax.axis_index("ctx")
    my_dp = lax.axis_index("dp")
    chips = n // 2
    chip = me // 2
    core = lax.rem(me, 2)
    partner = 2 * chip + 1 - core
    scale = hw ** (-0.5)
    rows = width // ndp
    qb = 256

    loads = []
    for i, (src, dst) in enumerate(((wt_hbm, wt), (wp_hbm, wp), (wproj_hbm, wproj), (wqkv_hbm, wqkv))):
        load = pltpu.make_async_copy(src, dst, load_sem.at[i])
        load.start()
        loads.append(load)

    barrier = pltpu.get_barrier_semaphore()
    for o in range(1, n):
        pl.semaphore_signal(barrier, inc=1, device_id=(my_dp, lax.rem(me + o, n)), device_id_type=MESH)
    for o in range(1, ndp):
        pl.semaphore_signal(barrier, inc=1, device_id=(lax.rem(my_dp + o, ndp), me), device_id_type=MESH)

    def cols(block):
        return pl.ds(pl.multiple_of(block * tokens, 128), tokens)

    def gather_copy(buf, which, slot, block, target):
        return pltpu.make_async_remote_copy(
            src_ref=buf.at[:, cols(block)], dst_ref=buf.at[:, cols(block)],
            send_sem=ag_send.at[which, slot], recv_sem=ag_recv.at[which, slot],
            device_id=(my_dp, target), device_id_type=MESH)

    def gather_start(buf, which):
        for o in range(1, chips):
            gather_copy(buf, which, o, me, 2 * lax.rem(chip + o, chips) + core).start()
        gather_copy(buf, which, 0, me, partner).start()

    def gather_finish(buf, which):
        for o in range(1, chips):
            source = lax.rem(chip - o + chips, chips)
            block = 2 * source + core
            gather_copy(buf, which, o, block, partner).wait_recv()
            gather_copy(buf, which, chips + o, block, partner).start()
        gather_copy(buf, which, 0, partner, partner).wait_recv()
        for o in range(1, chips):
            source = lax.rem(chip - o + chips, chips)
            gather_copy(buf, which, chips + o, 2 * source + 1 - core, partner).wait_recv()
        for o in range(chips):
            gather_copy(buf, which, o, me, partner).wait_send()
        for o in range(1, chips):
            gather_copy(buf, which, chips + o, me, partner).wait_send()

    survive = survive_ref[0, 0]
    normed, _ = normalize(x_ref[...].astype(f32))
    lin[:, cols(me)] = jnp.transpose(normed * gain_ref[...] + bias_ref[...]).astype(bf16)
    pl.semaphore_wait(barrier, n - 1 + ndp - 1)
    gather_start(lin, 0)
    branch_grad = (cot_ref[...].astype(f32) * survive).astype(bf16).astype(f32)
    gb[:, cols(me)] = jnp.transpose(branch_grad).astype(bf16)
    gather_start(gb, 1)
    proj_sum = jnp.sum(branch_grad, axis=0, keepdims=True)

    loads[0].wait()
    gather_finish(lin, 0)

    def project(i, carry):
        where = pl.ds(pl.multiple_of(i * qb, qb), qb)
        block = (nn(wt[...], lin[:, where]) + bqkv_ref[...]).astype(bf16)
        for p in range(3):
            for h in range(hh):
                r = (p * hh + h) * PAD
                piece = block[r:r + PAD]
                qkv[p, h, :, where] = piece
                tok[p, h, where, :] = turned(piece).astype(bf16)
        return carry

    lax.fori_loop(0, length // qb, project, 0)

    def forward(i, carry):
        h = lax.rem(i, hh)
        where = pl.ds(pl.multiple_of((i // hh) * qb, qb), qb)
        scores = nn(tok[1, h][:, :PAD], qkv[0, h, :, where]) * scale
        top = jnp.max(scores, axis=0, keepdims=True)
        grown = jnp.exp(scores - top)
        total = jnp.sum(grown, axis=0, keepdims=True)
        prob = grown * (1.0 / total)
        probs[h, :, where] = prob
        att[h, :, where] = nn(qkv[2, h], prob.astype(bf16)).astype(bf16)
        return carry

    lax.fori_loop(0, hh * (length // qb), forward, 0)

    def spread_copy(src, dst, o, ssem, rsem):
        target = lax.rem(me + o, n)
        lead = (slice(None),) * (len(src.shape) - 1)
        return pltpu.make_async_remote_copy(
            src_ref=src.at[lead + (cols(target),)], dst_ref=dst.at[me],
            send_sem=ssem.at[o], recv_sem=rsem.at[o],
            device_id=(my_dp, target), device_id_type=MESH)

    def spread_start(src, dst, ssem, rsem, slot):
        for o in range(1, n):
            spread_copy(src, dst, o, ssem, rsem).start()
        lead = (slice(None),) * (len(src.shape) - 1)
        own = pltpu.make_async_copy(src.at[lead + (cols(me),)], dst.at[me], own_sem.at[slot])
        own.start()
        return own

    def spread_finish(src, dst, ssem, rsem, own):
        own.wait()
        for o in range(1, n):
            spread_copy(src, dst, o, ssem, rsem).wait_send()
            source = lax.rem(me - o + n, n)
            lead = (slice(None),) * (len(src.shape) - 1)
            pltpu.make_async_remote_copy(
                src_ref=src.at[lead + (cols(source),)], dst_ref=dst.at[source],
                send_sem=ssem.at[o], recv_sem=rsem.at[o],
                device_id=(my_dp, source), device_id_type=MESH).wait_recv()

    att_own = spread_start(att, att_in, att_send, att_recv, 0)

    loads[1].wait()
    gather_finish(gb, 1)

    def project_back(i, carry):
        where = pl.ds(pl.multiple_of(i * qb, qb), qb)
        block = nn(wp[...], gb[:, where]).astype(bf16)
        for h in range(hh):
            piece = block[h * PAD:(h + 1) * PAD]
            ga[h, :, where] = piece
            gan[h, where, :] = turned(piece).astype(bf16)
        return carry

    lax.fori_loop(0, length // qb, project_back, 0)
    dkv[...] = jnp.zeros_like(dkv)

    def backward(i, carry):
        h = lax.rem(i, hh)
        where = pl.ds(pl.multiple_of((i // hh) * qb, qb), qb)
        prob = probs[h, :, where]
        grad = ga[h, :, where]
        delta = jnp.sum(grad.astype(f32) * att[h, :, where].astype(f32), axis=0, keepdims=True)
        grad_probs = nn(tok[2, h][:, :PAD], grad)
        grad_scores = (prob * (grad_probs - delta) * scale).astype(bf16)
        gt[0, h, :, where] = nn(qkv[1, h], grad_scores).astype(bf16)
        dkv[0, h] += nn(grad_scores, tok[0, h, where, :])
        dkv[1, h] += nn(prob.astype(bf16), gan[h, where, :])
        return carry

    lax.fori_loop(0, hh * (length // qb), backward, 0)
    for p in range(2):
        for h in range(hh):
            gt[1 + p, h] = jnp.transpose(dkv[p, h])[:PAD].astype(bf16)

    gt_own = spread_start(gt, gt_in, gt_send, gt_recv, 1)

    def rs_copy(part, o):
        target = lax.rem(my_dp + o, ndp)
        return pltpu.make_async_remote_copy(
            src_ref=rs_send.at[part, target], dst_ref=rs_recv.at[part, o],
            send_sem=rs_ssem.at[part, o], recv_sem=rs_rsem.at[part, o],
            device_id=(target, me), device_id_type=MESH)

    half = 2 * hh * PAD
    for part in range(2):
        for o in list(range(1, ndp)) + [0]:
            target = lax.rem(my_dp + o, ndp)
            where = pl.ds(pl.multiple_of(target * rows, 16), rows)
            if part == 0:
                block = jnp.concatenate([
                    nt(lin[where, :], gt[2].reshape(hh * PAD, length)),
                    nt(gb[where, :], att[...].reshape(hh * PAD, length))], axis=1)
            else:
                block = nt(lin[where, :], gt[0:2].reshape(half, length))
            rs_send[part, target] = (block * grad_scale).astype(bf16)
            if o:
                rs_copy(part, o).start()

    spread_finish(att, att_in, att_send, att_recv, att_own)
    attended = jnp.concatenate(
        [att_in[g, h].astype(f32)[:hw] for g in range(n) for h in range(hh)], axis=0)
    attended = jnp.transpose(attended).astype(bf16)
    loads[2].wait()
    branch = nn(attended, wproj[...]) + pbias_ref[...]
    out_ref[...] = (x_ref[...].astype(f32) + survive * branch).astype(bf16)

    spread_finish(gt, gt_in, gt_send, gt_recv, gt_own)
    for p in range(3):
        gp[p * width:(p + 1) * width, :] = jnp.concatenate(
            [gt_in[g, p, h].astype(f32)[:hw] for g in range(n) for h in range(hh)], axis=0).astype(bf16)
    loads[3].wait()

    def layer_rows(i, carry):
        where = pl.ds(pl.multiple_of(i * 128, 128), 128)
        glt[where, :] = nn(wqkv[where, :], gp[...])
        return carry

    lax.fori_loop(0, width // 128, layer_rows, 0)
    grad_layer = jnp.transpose(glt[...])
    normed, inv_scale = normalize(x_ref[...].astype(f32))
    ones = jnp.ones((8, tokens), bf16)
    terms = [
        jnp.sum(grad_layer * normed, axis=0, keepdims=True),
        jnp.sum(grad_layer, axis=0, keepdims=True),
        nt(ones, gp[0:width, :])[0:1],
        nt(ones, gp[2 * width:3 * width, :])[0:1],
        proj_sum,
        jnp.zeros((3, width), f32),
    ]
    terms = jnp.concatenate(terms, axis=0) * grad_scale
    for j in range(ndp):
        vec[j] = terms[:, j * rows:(j + 1) * rows]

    def vec_copy(o):
        target = lax.rem(my_dp + o, ndp)
        return pltpu.make_async_remote_copy(
            src_ref=vec.at[target], dst_ref=vec_in.at[o], send_sem=vs.at[o], recv_sem=vr.at[o],
            device_id=(target, me), device_id_type=MESH)

    for o in range(1, ndp):
        vec_copy(o).start()
    grad_norm = grad_layer * gain_ref[...]
    centre_term = jnp.mean(grad_norm, axis=-1, keepdims=True)
    slope_term = jnp.mean(grad_norm * normed, axis=-1, keepdims=True)
    gin_ref[...] = (
        cot_ref[...].astype(f32) + inv_scale * (grad_norm - centre_term - normed * slope_term)
    ).astype(bf16)

    total = vec[my_dp]
    for o in range(1, ndp):
        vec_copy(o).wait()
        total = total + vec_in[o]
    sums[...] = total

    def sum_copy(o):
        return pltpu.make_async_remote_copy(
            src_ref=sums, dst_ref=sums_in.at[o], send_sem=ss.at[o], recv_sem=sr.at[o],
            device_id=(my_dp, lax.rem(me + o, n)), device_id_type=MESH)

    for o in range(1, n):
        sum_copy(o).start()

    for part, dst in ((0, gvp_ref), (1, gqk_ref)):
        acc = rs_send[part, my_dp].astype(f32)
        for o in range(1, ndp):
            rs_copy(part, o).wait()
            acc = acc + rs_recv[part, o].astype(f32)
        dst[...] = acc

    for o in range(1, n):
        sum_copy(o).wait()
        total = total + sums_in[o]
    small_ref[...] = total


def local(inputs, cotangent, keep_mask, ln_gain, ln_bias, w_qkv, qv_bias, w_proj, proj_bias):
    samples, tokens, width = inputs.shape
    n = lax.axis_size("ctx")
    ndp = lax.axis_size("dp")
    hh = HEADS // n
    hw = width // HEADS
    length = tokens * n
    rows = width // ndp
    half = 2 * hh * PAD
    me = lax.axis_index("ctx")
    grad_scale = 1.0 / math.sqrt(samples * ndp * length)
    survive = (keep_mask.astype(f32) / keep_rate).reshape(1, 1)
    bias_full = jnp.concatenate([qv_bias[0], jnp.zeros_like(qv_bias[0]), qv_bias[1]])
    wt, bqkv, wp = [], [], []
    for p in range(3):
        for h in range(hh):
            start = p * width + (me * hh + h) * hw
            wt.append(jnp.pad(lax.dynamic_slice_in_dim(w_qkv, start, hw, 1).T, ((0, PAD - hw), (0, 0))))
            bqkv.append(jnp.pad(lax.dynamic_slice_in_dim(bias_full, start, hw), (0, PAD - hw)))
    for h in range(hh):
        piece = lax.dynamic_slice_in_dim(w_proj, (me * hh + h) * hw, hw, 0)
        wp.append(jnp.pad(piece, ((0, PAD - hw), (0, 0))))
    wt = jnp.concatenate(wt, axis=0)
    wp = jnp.concatenate(wp, axis=0)
    bqkv = jnp.concatenate(bqkv).reshape(3 * hh * PAD, 1)

    vmem = pl.BlockSpec(memory_space=pltpu.VMEM)
    hbm = pl.BlockSpec(memory_space=pl.ANY)
    dma = pltpu.SemaphoreType.DMA
    out, gin, gqk, gvp, small = pl.pallas_call(
        functools.partial(kernel, n, ndp, hh, hw, grad_scale),
        out_shape=(
            jax.ShapeDtypeStruct((tokens, width), bf16),
            jax.ShapeDtypeStruct((tokens, width), bf16),
            jax.ShapeDtypeStruct((rows, half), f32),
            jax.ShapeDtypeStruct((rows, half), f32),
            jax.ShapeDtypeStruct((8, rows), f32),
        ),
        in_specs=[pl.BlockSpec(memory_space=pltpu.SMEM)] + [vmem] * 6 + [hbm] * 4,
        out_specs=(vmem,) * 5,
        scratch_shapes=[
            pltpu.VMEM((3 * hh * PAD, width), bf16),
            pltpu.VMEM((hh * PAD, width), bf16),
            pltpu.VMEM((width, 3 * width), bf16),
            pltpu.VMEM((width, width), bf16),
            pltpu.VMEM((width, length), bf16),
            pltpu.VMEM((width, length), bf16),
            pltpu.VMEM((3, hh, PAD, length), bf16),
            pltpu.VMEM((3, hh, length, 128), bf16),
            pltpu.VMEM((hh, length, length), f32),
            pltpu.VMEM((hh, PAD, length), bf16),
            pltpu.VMEM((hh, PAD, length), bf16),
            pltpu.VMEM((hh, length, 128), bf16),
            pltpu.VMEM((2, hh, length, 128), f32),
            pltpu.VMEM((3, hh, PAD, length), bf16),
            pltpu.VMEM((n, hh, PAD, tokens), bf16),
            pltpu.VMEM((n, 3, hh, PAD, tokens), bf16),
            pltpu.VMEM((3 * width, tokens), bf16),
            pltpu.VMEM((width, tokens), f32),
            pltpu.VMEM((2, ndp, rows, half), bf16),
            pltpu.VMEM((2, ndp, rows, half), bf16),
            pltpu.VMEM((ndp, 8, rows), f32),
            pltpu.VMEM((ndp, 8, rows), f32),
            pltpu.VMEM((8, rows), f32),
            pltpu.VMEM((n, 8, rows), f32),
            dma((4,)), dma((2, n)), dma((2, n)), dma((n,)), dma((n,)), dma((n,)), dma((n,)),
            dma((2, ndp)), dma((2, ndp)), dma((ndp,)), dma((ndp,)), dma((n,)), dma((n,)), dma((2,)),
        ],
        compiler_params=pltpu.CompilerParams(
            collective_id=0, has_side_effects=True, vmem_limit_bytes=63 * 1024 * 1024),
    )(
        survive, inputs[0], cotangent[0], ln_gain[None], ln_bias[None], bqkv, proj_bias[None],
        wt, wp, w_qkv, w_proj,
    )
    def heads(block):
        return block.reshape(rows, hh, PAD)[:, :, :hw].reshape(rows, hh * hw)

    part = half // 2
    grad_w_qkv = jnp.stack(
        [heads(gqk[:, :part]), heads(gqk[:, part:]), heads(gvp[:, :part])], axis=1)
    grad_w_proj = heads(gvp[:, part:]).T
    own = rows // n
    mine = lax.dynamic_slice_in_dim(small, me * own, own, 1)
    return (
        out[None], gin[None], grad_w_qkv, grad_w_proj,
        mine[0], mine[1], mine[2:4], mine[4],
    )


def solution(mesh):
    placed = (P("dp", "ctx", None), P("dp", "ctx", None), P("dp"), P(), P(), P(), P(), P(), P())
    return jax.shard_map(
        local,
        mesh=mesh,
        in_specs=placed,
        out_specs=(
            P("dp", "ctx", None),
            P("dp", "ctx", None),
            P("dp", None, "ctx"),
            P("ctx", "dp"),
            P(("dp", "ctx")),
            P(("dp", "ctx")),
            P(None, ("dp", "ctx")),
            P(("dp", "ctx")),
        ),
        check_vma=False,
    )
```

profile of v0, /device:TPU:0, one launch (start us, length us, event | category | flops | bytes accessed | tf_op | source)
XLA Modules:
  0.0 128.8 jit_solution(13269245354729212597)
XLA Ops:
  0.6 3.1 %constant_dynamic-slice_fusion.3 = (bf16[1408,88]{1,0:T(8,128)(2,1)S(1)}, bf16[1408,88]{1,0:T(8,128)(2,1)S(1)}, bf16[1408,88]{1,0:T(8,128)(2,1)S(1)}, bf16[1408,...) fusion(bf16[1408,4224]{1,0:T(8,128)(2,1)} %wqkv_hbm.1, s32[]{:T(128)S(6)} %select_n.38, ...), kind=kLoop, calls=%fused_computation.18 | loop fusion | bytes 2973720 | tf_op jit(solution)/shard_map/dynamic_slice | solution.py:325
  3.7 0.2 copy.38
  3.9 0.7 pad_dynamic-update-slice_fusion.5
  4.6 0.2 copy.39
  4.8 0.7 pad_dynamic-update-slice_fusion.4
  5.5 0.2 copy.40
  5.7 0.7 pad_dynamic-update-slice_fusion.3
  6.4 0.0 copy-start.2
  6.4 0.2 copy.41
  6.6 0.7 pad_dynamic-update-slice_fusion.2
  7.3 0.2 copy.42
  7.5 0.7 pad_dynamic-update-slice_fusion.1
  8.3 0.2 copy.43
  8.4 0.0 copy-start.3
  8.5 0.0 copy-start.4
  8.5 0.0 copy-start.5
  8.5 0.7 pad_dynamic-update-slice_fusion.wt_hbm
  9.2 0.0 copy-done.2
  9.3 0.1 fusion.5
  9.4 0.1 concatenate.13
  9.5 0.9 reshape.44.bqkv_ref
  10.4 1.1 constant_dynamic-slice_fusion.2
  11.5 0.8 fusion.2.wp_hbm
  12.3 0.0 copy-done.3
  12.3 0.6 broadcast_in_dim.18.gain_ref
  12.9 0.0 copy-done.4
  12.9 0.6 broadcast_in_dim.19.bias_ref
  13.5 0.0 copy-done.5
  13.5 0.6 broadcast_in_dim.21.pbias_ref
  14.8 106.7 %shard_map.152 = (bf16[128,1408]{1,0:T(8,128)(2,1)}, bf16[128,1408]{1,0:T(8,128)(2,1)}, f32[352,384]{1,0:T(8,128)}, f32[352,384]{1,0:T(8,128)}, f32[8,352]{1,0:T(8,128)}) custom-call(f32[1,1]{1,0:T(1,128)} %bitcast.survive_ref, bf16[128,1408]{1,0:T(8,128)(2,1)} %bitcast.42, bf16[128,1408]{1,0:T(8,128)(2,1)} %bitcast.43, ...), custom_call_target="tpu_custom_call" | custom-call | tf_op jit(solution)/shard_map/pallas_call | solution.py:337
  121.5 1.6 %fusion.3 = (f32[352,192]{1,0:T(8,128)S(1)}, f32[352,192]{1,0:T(8,128)S(1)}, f32[352,192]{1,0:T(8,128)S(1)}, f32[352,192]{1,0:T(8,128)S(1)}) fusion(f32[352,384]{1,0:T(8,128)} %get-tuple-element.16, f32[352,384]{1,0:T(8,128)} %get-tuple-element.15), kind=kLoop, calls=%fused_computation.27 | loop fusion | bytes 2162688 | tf_op jit(solution)/shard_map/slice | solution.py:388
  123.0 0.1 copy.34
  123.2 0.1 copy.35
  123.4 0.1 copy.36
  123.6 0.0 copy-start.1
  123.6 0.0 copy-start
  123.6 0.9 pad_maximum_fusion
  124.6 0.1 copy.37
  124.7 0.7 slice.59
  125.4 0.8 constant_dynamic-slice_fusion
  126.2 0.5 slice_bitcast_fusion
  126.7 0.6 slice.54
  127.3 0.0 copy-done.1
  127.3 0.7 copy.52
  128.0 0.0 copy-done
  128.0 0.7 copy.53
  (12 shorter events, 0.1 us)
Async XLA Ops:
  6.4 2.8 %copy-start.2 = (f32[2,1408]{1,0:T(2,128)S(1)}, f32[2,1408]{1,0:T(2,128)}, u32[]{:S(2)}) copy-start(f32[2,1408]{1,0:T(2,128)} %param.15) | copy-start | bytes 33796
  8.4 3.9 %copy-start.3 = (f32[1408]{0:T(1024)S(1)}, f32[1408]{0:T(1024)}, u32[]{:S(2)}) copy-start(f32[1408]{0:T(1024)} %param.12) | copy-start | bytes 16900
  8.5 4.5 %copy-start.4 = (f32[1408]{0:T(1024)S(1)}, f32[1408]{0:T(1024)}, u32[]{:S(2)}) copy-start(f32[1408]{0:T(1024)} %param.13) | copy-start | bytes 16900
  8.5 5.1 %copy-start.5 = (f32[1408]{0:T(1024)S(1)}, f32[1408]{0:T(1024)}, u32[]{:S(2)}) copy-start(f32[1408]{0:T(1024)} %param.17) | copy-start | bytes 16900
  123.6 3.7 %copy-start.1 = (bf16[128,1408]{1,0:T(8,128)(2,1)S(1)}, bf16[128,1408]{1,0:T(8,128)(2,1)}, u32[]{:S(2)}) copy-start(bf16[128,1408]{1,0:T(8,128)(2,1)} %get-tuple-element.13) | copy-start | bytes 1081348
  123.6 4.4 %copy-start = (bf16[128,1408]{1,0:T(8,128)(2,1)S(1)}, bf16[128,1408]{1,0:T(8,128)(2,1)}, u32[]{:S(2)}) copy-start(bf16[128,1408]{1,0:T(8,128)(2,1)} %get-tuple-element.14) | copy-start | bytes 1081348
where the time goes:
time: 129 us
  Pallas kernels  107 us (83%)
  local copies, waits for them, and re-layouts  18.8 us (15%)
  other arithmetic  1.79 us (1%)
  between operations  1.49 us (1%)
    pallas_call x1, Pallas kernels, local(): pl.pallas_call(functools.partial(kernel, n, ndp, hh, hw, grad_scale), out...  107 us
    unnamed x25, local copies, waits for them, and re-layouts  6.22 us
    dynamic_slice x1, local copies, waits for them, and re-layouts, local(): lax.dynamic_slice_in_dim(w_qkv, start, hw, 1)  3.06 us

commit v1 on v0

v1 whole, which is shorter than its diff:
```python
import functools
import math

import jax
import jax.numpy as jnp
from jax import lax
from jax.experimental import pallas as pl
from jax.experimental.pallas import tpu as pltpu
from jax.sharding import PartitionSpec as P

HEADS = 16
PAD = 96
eps = 1e-06
keep_rate = 0.75
MESH = pl.DeviceIdType.MESH
f32 = jnp.float32
bf16 = jnp.bfloat16


def nt(left, right):
    return lax.dot_general(left, right, (((1,), (1,)), ((), ())), preferred_element_type=f32)


def nn(left, right):
    return jnp.dot(left, right, preferred_element_type=f32)


def turned(block):
    wide = block.astype(f32)
    fill = jnp.zeros((128 - PAD, wide.shape[1]), f32)
    return jnp.transpose(jnp.concatenate([wide, fill], axis=0))


def normalize(values):
    average = jnp.mean(values, axis=-1, keepdims=True)
    centred = values - average
    variance = jnp.mean(centred * centred, axis=-1, keepdims=True)
    inv_scale = lax.rsqrt(variance + eps)
    return centred * inv_scale, inv_scale


def kernel(
    n, ndp, hh, hw, grad_scale,
    survive_ref, x_ref, cot_ref, gain_ref, bias_ref, qvb_ref, pbias_ref,
    wqkv_hbm, wproj_hbm,
    out_ref, gin_ref, gproj_ref, gqkv_ref, small_ref,
    wt, wp, bqkv_ref, wqkv, wproj, lin, gb, qkv, tok, probs, att, ga, gan, dkv, gt,
    att_in, gt_in, gp, glt, ps_send, ps_recv, rs_send, rs_recv, vec, vec_in, sums, sums_in,
    load_sem, ag_send, ag_recv, att_send, att_recv, gt_send, gt_recv,
    ps_ssem, ps_rsem, rs_ssem, rs_rsem, vs, vr, ss, sr, own_sem,
):
    tokens, width = x_ref.shape
    length = tokens * n
    me = lax.axis_index("ctx")
    my_dp = lax.axis_index("dp")
    chips = n // 2
    chip = me // 2
    core = lax.rem(me, 2)
    partner = 2 * chip + 1 - core
    scale = hw ** (-0.5)
    rows = width // ndp
    qb = 256

    loads = []
    for i, (src, dst) in enumerate(((wqkv_hbm, wqkv), (wproj_hbm, wproj))):
        load = pltpu.make_async_copy(src, dst, load_sem.at[i])
        load.start()
        loads.append(load)

    barrier = pltpu.get_barrier_semaphore()
    for o in range(1, n):
        pl.semaphore_signal(barrier, inc=1, device_id=(my_dp, lax.rem(me + o, n)), device_id_type=MESH)
    for o in range(1, ndp):
        pl.semaphore_signal(barrier, inc=1, device_id=(lax.rem(my_dp + o, ndp), me), device_id_type=MESH)

    def cols(block):
        return pl.ds(pl.multiple_of(block * tokens, 128), tokens)

    def gather_copy(buf, which, slot, block, target):
        return pltpu.make_async_remote_copy(
            src_ref=buf.at[:, cols(block)], dst_ref=buf.at[:, cols(block)],
            send_sem=ag_send.at[which, slot], recv_sem=ag_recv.at[which, slot],
            device_id=(my_dp, target), device_id_type=MESH)

    square = chips == 4
    if square:
        along_x = chip + 1 - 2 * lax.rem(chip, 2)
        along_y = lax.rem(chip + 2, 4)
        onward = along_x * (1 - core) + along_y * core
        inward = along_y * (1 - core) + along_x * core
        sources = [None, inward, onward, 3 - chip]
        targets = [None, inward, onward]
    else:
        sources = [None] + [lax.rem(chip - o + chips, chips) for o in range(1, chips)]
        targets = [None] + [lax.rem(chip + o, chips) for o in range(1, chips)]

    def gather_start(buf, which):
        for o in range(1, len(targets)):
            gather_copy(buf, which, o, me, 2 * targets[o] + core).start()
        gather_copy(buf, which, 0, me, partner).start()

    def gather_step(buf, which, o):
        block = 2 * sources[o] + core
        gather_copy(buf, which, o, block, partner).wait_recv()
        if square and o == 1:
            gather_copy(buf, which, 3, block, 2 * onward + core).start()
        gather_copy(buf, which, chips + o, block, partner).start()

    def gather_finish(buf, which):
        gather_copy(buf, which, 0, partner, partner).wait_recv()
        for o in range(1, chips):
            gather_copy(buf, which, chips + o, 2 * sources[o] + 1 - core, partner).wait_recv()
        for o in range(chips):
            gather_copy(buf, which, o, me, partner).wait_send()
        for o in range(1, chips):
            gather_copy(buf, which, chips + o, me, partner).wait_send()

    survive = survive_ref[0, 0]
    normed, _ = normalize(x_ref[...].astype(f32))
    lin[:, cols(me)] = jnp.transpose(normed * gain_ref[...] + bias_ref[...]).astype(bf16)
    pl.semaphore_wait(barrier, n - 1 + ndp - 1)
    gather_start(lin, 0)
    branch_grad = (cot_ref[...].astype(f32) * survive).astype(bf16).astype(f32)
    gb[:, cols(me)] = jnp.transpose(branch_grad).astype(bf16)
    proj_sum = jnp.sum(branch_grad, axis=0, keepdims=True)

    row_id = lax.broadcasted_iota(jnp.int32, (PAD, 256), 0)
    col_id = lax.broadcasted_iota(jnp.int32, (PAD, 256), 1)
    row_sq = lax.broadcasted_iota(jnp.int32, (PAD, PAD), 0)
    col_sq = lax.broadcasted_iota(jnp.int32, (PAD, PAD), 1)
    loads[0].wait()
    for h in range(hh):
        off = (me * hh + h) * hw
        begin = (off // 128) * 128
        begin = begin - 128 * (begin // (width - 128))
        pick = (col_id == row_id + (off - begin)) & (row_id < hw)
        ones_at = jnp.where(pick, 1.0, 0.0)
        for p in range(3):
            r = (p * hh + h) * PAD
            window = wqkv[:, pl.ds(pl.multiple_of(p * width + begin, 128), 256)]
            wt[r:r + PAD, :] = nt(ones_at.astype(bf16), window).astype(bf16)
            if p == 1:
                bqkv_ref[r:r + PAD, :] = jnp.zeros((PAD, 1), f32)
            else:
                entries = qvb_ref[p // 2:p // 2 + 1, pl.ds(pl.multiple_of(begin, 128), 256)]
                bqkv_ref[r:r + PAD, :] = jnp.sum(
                    jnp.where(pick, entries, 0.0), axis=1, keepdims=True)
    for o in range(1, len(targets)):
        gather_step(lin, 0, o)
    gather_start(gb, 1)
    for o in range(len(targets), chips):
        gather_step(lin, 0, o)
    loads[1].wait()
    for h in range(hh):
        off = (me * hh + h) * hw
        begin = (off // 16) * 16
        pick = (col_sq == row_sq + (off - begin)) & (row_sq < hw)
        window = wproj[pl.ds(pl.multiple_of(begin, 16), PAD), :]
        wp[h * PAD:(h + 1) * PAD, :] = nn(jnp.where(pick, 1.0, 0.0).astype(bf16), window).astype(bf16)
    gather_finish(lin, 0)

    def project(i, carry):
        where = pl.ds(pl.multiple_of(i * qb, qb), qb)
        block = (nn(wt[...], lin[:, where]) + bqkv_ref[...]).astype(bf16)
        for p in range(3):
            for h in range(hh):
                r = (p * hh + h) * PAD
                piece = block[r:r + PAD]
                qkv[p, h, :, where] = piece
                tok[p, h, where, :] = turned(piece).astype(bf16)
        return carry

    lax.fori_loop(0, length // qb, project, 0)
    gather_step(gb, 1, 1)

    def forward(i, carry):
        h = lax.rem(i, hh)
        where = pl.ds(pl.multiple_of((i // hh) * qb, qb), qb)
        scores = nn(tok[1, h][:, :PAD], qkv[0, h, :, where]) * scale
        top = jnp.max(scores, axis=0, keepdims=True)
        grown = jnp.exp(scores - top)
        total = jnp.sum(grown, axis=0, keepdims=True)
        prob = grown * (1.0 / total)
        probs[h, :, where] = prob
        att[h, :, where] = nn(qkv[2, h], prob.astype(bf16)).astype(bf16)
        return carry

    lax.fori_loop(0, hh * (length // qb), forward, 0)

    def spread_copy(src, dst, o, ssem, rsem, lanes, slot, target):
        lead = (slice(None),) * (len(src.shape) - 1)
        return pltpu.make_async_remote_copy(
            src_ref=src.at[lead + (cols(lanes),)], dst_ref=dst.at[slot],
            send_sem=ssem.at[o], recv_sem=rsem.at[o],
            device_id=(my_dp, target), device_id_type=MESH)

    def spread_start(src, dst, ssem, rsem, own_slot):
        for o in range(1, n):
            target = lax.rem(me + o, n)
            spread_copy(src, dst, o, ssem, rsem, target, me, target).start()
        lead = (slice(None),) * (len(src.shape) - 1)
        own = pltpu.make_async_copy(src.at[lead + (cols(me),)], dst.at[me], own_sem.at[own_slot])
        own.start()
        return own

    def spread_finish(src, dst, ssem, rsem, own):
        own.wait()
        for o in range(1, n):
            target = lax.rem(me + o, n)
            source = lax.rem(me - o + n, n)
            spread_copy(src, dst, o, ssem, rsem, target, me, target).wait_send()
            spread_copy(src, dst, o, ssem, rsem, source, source, source).wait_recv()

    for o in range(2, chips):
        gather_step(gb, 1, o)
    att_own = spread_start(att, att_in, att_send, att_recv, 0)

    gather_finish(gb, 1)

    def project_back(i, carry):
        where = pl.ds(pl.multiple_of(i * qb, qb), qb)
        block = nn(wp[...], gb[:, where]).astype(bf16)
        for h in range(hh):
            piece = block[h * PAD:(h + 1) * PAD]
            ga[h, :, where] = piece
            gan[h, where, :] = turned(piece).astype(bf16)
        return carry

    lax.fori_loop(0, length // qb, project_back, 0)
    def ps_copy(o):
        target = lax.rem(my_dp + o, ndp)
        return pltpu.make_async_remote_copy(
            src_ref=ps_send.at[target], dst_ref=ps_recv.at[o],
            send_sem=ps_ssem.at[o], recv_sem=ps_rsem.at[o],
            device_id=(target, me), device_id_type=MESH)

    def rs_copy(h, o):
        target = lax.rem(my_dp + o, ndp)
        return pltpu.make_async_remote_copy(
            src_ref=rs_send.at[h, target], dst_ref=rs_recv.at[h, o],
            send_sem=rs_ssem.at[h, o], recv_sem=rs_rsem.at[h, o],
            device_id=(target, me), device_id_type=MESH)

    order = list(range(1, ndp)) + [0]

    def compact(pieces, to):
        pieces = [piece.astype(f32)[:hw] for piece in pieces]
        more = to - hw * len(pieces)
        if more:
            pieces.append(jnp.zeros((more, length), f32))
        return jnp.concatenate(pieces, axis=0).astype(bf16)

    left = compact([att[h] for h in range(hh)], ps_send.shape[1])
    for o in order:
        target = lax.rem(my_dp + o, ndp)
        where = pl.ds(pl.multiple_of(target * rows, 16), rows)
        ps_send[target] = (nt(left, gb[where, :]) * grad_scale).astype(bf16)
        if o:
            ps_copy(o).start()

    dkv[...] = jnp.zeros_like(dkv)
    gt_owns = []
    for h in range(hh):
        def backward(i, carry, h=h):
            where = pl.ds(pl.multiple_of(i * qb, qb), qb)
            prob = probs[h, :, where]
            grad = ga[h, :, where]
            delta = jnp.sum(grad.astype(f32) * att[h, :, where].astype(f32), axis=0, keepdims=True)
            grad_probs = nn(tok[2, h][:, :PAD], grad)
            grad_scores = (prob * (grad_probs - delta) * scale).astype(bf16)
            gt[h, 0, :, where] = nn(qkv[1, h], grad_scores).astype(bf16)
            dkv[0, h] += nn(grad_scores, tok[0, h, where, :])
            dkv[1, h] += nn(prob.astype(bf16), gan[h, where, :])
            return carry

        lax.fori_loop(0, length // qb, backward, 0)
        for p in range(2):
            gt[h, 1 + p] = jnp.transpose(dkv[p, h])[:PAD].astype(bf16)
        gt_owns.append(spread_start(gt.at[h], gt_in.at[h], gt_send.at[h], gt_recv.at[h], 1 + h))
        left = compact([gt[h, p] for p in range(3)], rs_send.shape[2])
        for o in order:
            target = lax.rem(my_dp + o, ndp)
            where = pl.ds(pl.multiple_of(target * rows, 16), rows)
            rs_send[h, target] = (nt(left, lin[where, :]) * grad_scale).astype(bf16)
            if o:
                rs_copy(h, o).start()

    spread_finish(att, att_in, att_send, att_recv, att_own)
    attended = jnp.concatenate(
        [att_in[g, h].astype(f32)[:hw] for g in range(n) for h in range(hh)], axis=0)
    attended = jnp.transpose(attended).astype(bf16)
    branch = nn(attended, wproj[...]) + pbias_ref[...]
    out_ref[...] = (x_ref[...].astype(f32) + survive * branch).astype(bf16)

    for h in range(hh):
        spread_finish(gt.at[h], gt_in.at[h], gt_send.at[h], gt_recv.at[h], gt_owns[h])
    for p in range(3):
        gp[p * width:(p + 1) * width, :] = jnp.concatenate(
            [gt_in[h, g, p].astype(f32)[:hw] for g in range(n) for h in range(hh)], axis=0).astype(bf16)

    def layer_rows(i, carry):
        where = pl.ds(pl.multiple_of(i * 128, 128), 128)
        glt[where, :] = nn(wqkv[where, :], gp[...])
        return carry

    lax.fori_loop(0, width // 128, layer_rows, 0)
    grad_layer = jnp.transpose(glt[...])
    normed, inv_scale = normalize(x_ref[...].astype(f32))
    ones = jnp.ones((8, tokens), bf16)
    terms = [
        jnp.sum(grad_layer * normed, axis=0, keepdims=True),
        jnp.sum(grad_layer, axis=0, keepdims=True),
        nt(ones, gp[0:width, :])[0:1],
        nt(ones, gp[2 * width:3 * width, :])[0:1],
        proj_sum,
        jnp.zeros((3, width), f32),
    ]
    terms = jnp.concatenate(terms, axis=0) * grad_scale
    for j in range(ndp):
        vec[j] = terms[:, j * rows:(j + 1) * rows]

    def vec_copy(o):
        target = lax.rem(my_dp + o, ndp)
        return pltpu.make_async_remote_copy(
            src_ref=vec.at[target], dst_ref=vec_in.at[o], send_sem=vs.at[o], recv_sem=vr.at[o],
            device_id=(target, me), device_id_type=MESH)

    for o in range(1, ndp):
        vec_copy(o).start()
    grad_norm = grad_layer * gain_ref[...]
    centre_term = jnp.mean(grad_norm, axis=-1, keepdims=True)
    slope_term = jnp.mean(grad_norm * normed, axis=-1, keepdims=True)
    gin_ref[...] = (
        cot_ref[...].astype(f32) + inv_scale * (grad_norm - centre_term - normed * slope_term)
    ).astype(bf16)

    total = vec[my_dp]
    for o in range(1, ndp):
        vec_copy(o).wait()
        total = total + vec_in[o]
    sums[...] = total

    def sum_copy(o):
        return pltpu.make_async_remote_copy(
            src_ref=sums, dst_ref=sums_in.at[o], send_sem=ss.at[o], recv_sem=sr.at[o],
            device_id=(my_dp, lax.rem(me + o, n)), device_id_type=MESH)

    for o in range(1, n):
        sum_copy(o).start()

    acc = ps_send[my_dp].astype(f32)
    for o in range(1, ndp):
        ps_copy(o).wait()
        acc = acc + ps_recv[o].astype(f32)
    gproj_ref[...] = acc
    for h in range(hh):
        acc = rs_send[h, my_dp].astype(f32)
        for o in range(1, ndp):
            rs_copy(h, o).wait()
            acc = acc + rs_recv[h, o].astype(f32)
        gqkv_ref[h] = acc

    for o in range(1, n):
        sum_copy(o).wait()
        total = total + sums_in[o]
    small_ref[...] = total


def local(inputs, cotangent, keep_mask, ln_gain, ln_bias, w_qkv, qv_bias, w_proj, proj_bias):
    samples, tokens, width = inputs.shape
    n = lax.axis_size("ctx")
    ndp = lax.axis_size("dp")
    hh = HEADS // n
    hw = width // HEADS
    length = tokens * n
    rows = width // ndp
    across = -(-hh * hw // 16) * 16
    tall = -(-3 * hw // 16) * 16
    me = lax.axis_index("ctx")
    grad_scale = 1.0 / math.sqrt(samples * ndp * length)
    survive = (keep_mask.astype(f32) / keep_rate).reshape(1, 1)
    vmem = pl.BlockSpec(memory_space=pltpu.VMEM)
    hbm = pl.BlockSpec(memory_space=pl.ANY)
    dma = pltpu.SemaphoreType.DMA
    out, gin, gproj, gqkv, small = pl.pallas_call(
        functools.partial(kernel, n, ndp, hh, hw, grad_scale),
        out_shape=(
            jax.ShapeDtypeStruct((tokens, width), bf16),
            jax.ShapeDtypeStruct((tokens, width), bf16),
            jax.ShapeDtypeStruct((across, rows), f32),
            jax.ShapeDtypeStruct((hh, tall, rows), f32),
            jax.ShapeDtypeStruct((8, rows), f32),
        ),
        in_specs=[pl.BlockSpec(memory_space=pltpu.SMEM)] + [vmem] * 6 + [hbm] * 2,
        out_specs=(vmem,) * 5,
        scratch_shapes=[
            pltpu.VMEM((3 * hh * PAD, width), bf16),
            pltpu.VMEM((hh * PAD, width), bf16),
            pltpu.VMEM((3 * hh * PAD, 1), f32),
            pltpu.VMEM((width, 3 * width), bf16),
            pltpu.VMEM((width, width), bf16),
            pltpu.VMEM((width, length), bf16),
            pltpu.VMEM((width, length), bf16),
            pltpu.VMEM((3, hh, PAD, length), bf16),
            pltpu.VMEM((3, hh, length, 128), bf16),
            pltpu.VMEM((hh, length, length), f32),
            pltpu.VMEM((hh, PAD, length), bf16),
            pltpu.VMEM((hh, PAD, length), bf16),
            pltpu.VMEM((hh, length, 128), bf16),
            pltpu.VMEM((2, hh, length, 128), f32),
            pltpu.VMEM((hh, 3, PAD, length), bf16),
            pltpu.VMEM((n, hh, PAD, tokens), bf16),
            pltpu.VMEM((hh, n, 3, PAD, tokens), bf16),
            pltpu.VMEM((3 * width, tokens), bf16),
            pltpu.VMEM((width, tokens), f32),
            pltpu.VMEM((ndp, across, rows), bf16),
            pltpu.VMEM((ndp, across, rows), bf16),
            pltpu.VMEM((hh, ndp, tall, rows), bf16),
            pltpu.VMEM((hh, ndp, tall, rows), bf16),
            pltpu.VMEM((ndp, 8, rows), f32),
            pltpu.VMEM((ndp, 8, rows), f32),
            pltpu.VMEM((8, rows), f32),
            pltpu.VMEM((n, 8, rows), f32),
            dma((2,)), dma((2, n)), dma((2, n)), dma((n,)), dma((n,)), dma((hh, n)), dma((hh, n)),
            dma((ndp,)), dma((ndp,)), dma((hh, ndp)), dma((hh, ndp)),
            dma((ndp,)), dma((ndp,)), dma((n,)), dma((n,)), dma((1 + hh,)),
        ],
        compiler_params=pltpu.CompilerParams(
            collective_id=0, has_side_effects=True, vmem_limit_bytes=63 * 1024 * 1024),
    )(
        survive, inputs[0], cotangent[0], ln_gain[None], ln_bias[None], qv_bias, proj_bias[None],
        w_qkv, w_proj,
    )
    grad_w_qkv = gqkv[:, :3 * hw].reshape(hh, 3, hw, rows).transpose(3, 1, 0, 2).reshape(rows, 3, hh * hw)
    grad_w_proj = gproj[:hh * hw]
    own = rows // n
    mine = lax.dynamic_slice_in_dim(small, me * own, own, 1)
    return (
        out[None], gin[None], grad_w_qkv, grad_w_proj,
        mine[0], mine[1], mine[2:4], mine[4],
    )


def solution(mesh):
    placed = (P("dp", "ctx", None), P("dp", "ctx", None), P("dp"), P(), P(), P(), P(), P(), P())
    return jax.shard_map(
        local,
        mesh=mesh,
        in_specs=placed,
        out_specs=(
            P("dp", "ctx", None),
            P("dp", "ctx", None),
            P("dp", None, "ctx"),
            P("ctx", "dp"),
            P(("dp", "ctx")),
            P(("dp", "ctx")),
            P(None, ("dp", "ctx")),
            P(("dp", "ctx")),
        ),
        check_vma=False,
    )
```

time: 129 us -> 113 us (0.88)
  Pallas kernels: 107 us -> 98.3 us
  local copies, waits for them, and re-layouts: 18.8 us -> 13 us
  other arithmetic: 1.79 us -> 0 us
    pallas_call x1, Pallas kernels: 107 us -> 98.3 us  [local(): pl.pallas_call(functools.partial(kernel, n, ndp, hh, hw, grad_scale), out...]
    dynamic_slice x3 -> x0, local copies, waits for them, and re-layouts: 4.27 us -> none  [the longest x1 3.06 us: local(): lax.dynamic_slice_in_dim(w_qkv, start, hw, 1)]
    slice x10 -> x1, local copies, waits for them, and re-layouts: 2.96 us -> 1.19 us  [local(): gqkv[:, :3 * hw].reshape(hh, 3, hw, rows).transpose(3, 1, 0, 2)]
    unnamed x25 -> x3, local copies, waits for them, and re-layouts: 6.22 us -> 5.16 us
where the time goes in v1:
time: 113 us
  Pallas kernels  98.3 us (87%)
  local copies, waits for them, and re-layouts  13 us (12%)
  between operations  1.3 us (1%)
    pallas_call x1, Pallas kernels, local(): pl.pallas_call(functools.partial(kernel, n, ndp, hh, hw, grad_scale), out...  98.3 us
    unnamed x3, local copies, waits for them, and re-layouts  5.16 us

profile of v1, /device:TPU:0, one launch (start us, length us, event | category | flops | bytes accessed | tf_op | source)
XLA Modules:
  0.0 112.7 jit_solution(14688253722669492623)
XLA Ops:
  1.3 1.3 %broadcast_in_dim.15.gain_ref = f32[1,1408]{1,0:T(1,128)} reshape(f32[1408]{0:T(1024)} %param.12) | data formatting | bytes 11264 | tf_op jit(solution)/shard_map/broadcast_in_dim | solution.py:431
  2.6 1.3 %broadcast_in_dim.16.bias_ref = f32[1,1408]{1,0:T(1,128)} reshape(f32[1408]{0:T(1024)} %param.13) | data formatting | bytes 11264 | tf_op jit(solution)/shard_map/broadcast_in_dim | solution.py:431
  3.9 1.3 %broadcast_in_dim.17.pbias_ref = f32[1,1408]{1,0:T(1,128)} reshape(f32[1408]{0:T(1024)} %param.17) | data formatting | bytes 11264 | tf_op jit(solution)/shard_map/broadcast_in_dim | solution.py:431
  5.2 98.3 %shard_map.152 = (bf16[128,1408]{1,0:T(8,128)(2,1)}, bf16[128,1408]{1,0:T(8,128)(2,1)}, f32[176,352]{1,0:T(8,128)}, f32[2,272,352]{2,1,0:T(8,128)}, f32[8,352]{1,0:T(8,128)}) custom-call(f32[1,1]{1,0:T(1,128)} %bitcast.survive_ref, bf16[128,1408]{1,0:T(8,128)(2,1)} %bitcast.19, bf16[128,1408]{1,0:T(8,128)(2,1)} %bitcast.20, ...), custom_call_target="tpu_custom_call" | custom-call | tf_op jit(solution)/shard_map/pallas_call | solution.py:385
  103.5 0.8 constant_dynamic-slice_fusion
  104.3 0.6 slice.18
  104.9 0.5 slice_bitcast_fusion
  105.4 1.2 %slice.15 = f32[2,264,352]{2,1,0:T(8,128)S(1)} slice(f32[2,272,352]{2,1,0:T(8,128)} %get-tuple-element.15), slice={[0:2], [0:264], [0:352]} | slice | bytes 1486848 | tf_op jit(solution)/shard_map/slice | solution.py:434
  106.6 0.9 copy.17
  107.5 1.7 %copy.22 = bf16[1,128,1408]{2,1,0:T(8,128)(2,1)} copy(bf16[1,128,1408]{2,1,0:T(8,128)(2,1)} %bitcast.18) | data formatting | bytes 720896
  109.3 1.7 %copy.23 = bf16[1,128,1408]{2,1,0:T(8,128)(2,1)} copy(bf16[1,128,1408]{2,1,0:T(8,128)(2,1)} %bitcast.17) | data formatting | bytes 720896
  111.0 1.7 %copy.24 = f32[176,352]{1,0:T(8,128)} copy(f32[176,352]{1,0:T(8,128)} %get-tuple-element.32) | data formatting | bytes 495616

commit v2 on v1

--- a/solution.py
+++ b/solution.py
@@ -117,7 +117,7 @@
 
     survive = survive_ref[0, 0]
     normed, _ = normalize(x_ref[...].astype(f32))
-    lin[:, cols(me)] = jnp.transpose(normed * gain_ref[...] + bias_ref[...]).astype(bf16)
+    lin[:, cols(me)] = jnp.transpose(normed * gain_ref[...].reshape(1, width) + bias_ref[...].reshape(1, width)).astype(bf16)
     pl.semaphore_wait(barrier, n - 1 + ndp - 1)
     gather_start(lin, 0)
     branch_grad = (cot_ref[...].astype(f32) * survive).astype(bf16).astype(f32)
@@ -227,21 +227,55 @@
         return carry
 
     lax.fori_loop(0, length // qb, project_back, 0)
-    def ps_copy(o):
-        target = lax.rem(my_dp + o, ndp)
+    parts = [(ps_send, ps_recv, ps_ssem, ps_rsem)] + [
+        (rs_send.at[h], rs_recv.at[h], rs_ssem.at[h], rs_rsem.at[h]) for h in range(hh)]
+    halving = ndp == 4
+    parity = lax.rem(my_dp, 2)
+    beside = my_dp + 1 - 2 * parity
+    far = lax.rem(my_dp + 2, ndp)
+
+    def reduce_copy(part, k):
+        send, recv, ssem, rsem = parts[part]
+        if not halving:
+            block = target = lax.rem(my_dp + k, ndp)
+        elif k < 2:
+            block, target = 1 - parity + 2 * k, beside
+        else:
+            block = target = far
         return pltpu.make_async_remote_copy(
-            src_ref=ps_send.at[target], dst_ref=ps_recv.at[o],
-            send_sem=ps_ssem.at[o], recv_sem=ps_rsem.at[o],
+            src_ref=send.at[block], dst_ref=recv.at[k],
+            send_sem=ssem.at[k], recv_sem=rsem.at[k],
             device_id=(target, me), device_id_type=MESH)
 
-    def rs_copy(h, o):
-        target = lax.rem(my_dp + o, ndp)
-        return pltpu.make_async_remote_copy(
-            src_ref=rs_send.at[h, target], dst_ref=rs_recv.at[h, o],
-            send_sem=rs_ssem.at[h, o], recv_sem=rs_rsem.at[h, o],
-            device_id=(target, me), device_id_type=MESH)
-
-    order = list(range(1, ndp)) + [0]
+    def reduce_first(part, left, buf):
+        if halving:
+            order = [(1 - parity, 0), (3 - parity, 1), (parity, None), (parity + 2, None)]
+        else:
+            order = [(lax.rem(my_dp + o, ndp), o) for o in range(1, ndp)] + [(my_dp, None)]
+        for block, k in order:
+            where = pl.ds(pl.multiple_of(block * rows, 16), rows)
+            parts[part][0][block] = (nt(left, buf[where, :]) * grad_scale).astype(bf16)
+            if k is not None:
+                reduce_copy(part, k).start()
+
+    def reduce_second(part):
+        if halving:
+            send, recv, _, _ = parts[part]
+            for k in range(2):
+                reduce_copy(part, k).wait()
+            send[far] = (send[far].astype(f32) + recv[far // 2].astype(f32)).astype(bf16)
+            reduce_copy(part, 2).start()
+
+    def reduce_last(part):
+        send, recv, _, _ = parts[part]
+        acc = send[my_dp].astype(f32)
+        if halving:
+            reduce_copy(part, 2).wait()
+            return acc + recv[my_dp // 2].astype(f32) + recv[2].astype(f32)
+        for o in range(1, ndp):
+            reduce_copy(part, o).wait()
+            acc = acc + recv[o].astype(f32)
+        return acc
 
     def compact(pieces, to):
         pieces = [piece.astype(f32)[:hw] for piece in pieces]
@@ -251,12 +285,7 @@
         return jnp.concatenate(pieces, axis=0).astype(bf16)
 
     left = compact([att[h] for h in range(hh)], ps_send.shape[1])
-    for o in order:
-        target = lax.rem(my_dp + o, ndp)
-        where = pl.ds(pl.multiple_of(target * rows, 16), rows)
-        ps_send[target] = (nt(left, gb[where, :]) * grad_scale).astype(bf16)
-        if o:
-            ps_copy(o).start()
+    reduce_first(0, left, gb)
 
     dkv[...] = jnp.zeros_like(dkv)
     gt_owns = []
@@ -278,18 +307,14 @@
             gt[h, 1 + p] = jnp.transpose(dkv[p, h])[:PAD].astype(bf16)
         gt_owns.append(spread_start(gt.at[h], gt_in.at[h], gt_send.at[h], gt_recv.at[h], 1 + h))
         left = compact([gt[h, p] for p in range(3)], rs_send.shape[2])
-        for o in order:
-            target = lax.rem(my_dp + o, ndp)
-            where = pl.ds(pl.multiple_of(target * rows, 16), rows)
-            rs_send[h, target] = (nt(left, lin[where, :]) * grad_scale).astype(bf16)
-            if o:
-                rs_copy(h, o).start()
+        reduce_first(1 + h, left, lin)
+        reduce_second(h)
 
     spread_finish(att, att_in, att_send, att_recv, att_own)
     attended = jnp.concatenate(
         [att_in[g, h].astype(f32)[:hw] for g in range(n) for h in range(hh)], axis=0)
     attended = jnp.transpose(attended).astype(bf16)
-    branch = nn(attended, wproj[...]) + pbias_ref[...]
+    branch = nn(attended, wproj[...]) + pbias_ref[...].reshape(1, width)
     out_ref[...] = (x_ref[...].astype(f32) + survive * branch).astype(bf16)
 
     for h in range(hh):
@@ -304,6 +329,7 @@
         return carry
 
     lax.fori_loop(0, width // 128, layer_rows, 0)
+    reduce_second(hh)
     grad_layer = jnp.transpose(glt[...])
     normed, inv_scale = normalize(x_ref[...].astype(f32))
     ones = jnp.ones((8, tokens), bf16)
@@ -327,7 +353,7 @@
 
     for o in range(1, ndp):
         vec_copy(o).start()
-    grad_norm = grad_layer * gain_ref[...]
+    grad_norm = grad_layer * gain_ref[...].reshape(1, width)
     centre_term = jnp.mean(grad_norm, axis=-1, keepdims=True)
     slope_term = jnp.mean(grad_norm * normed, axis=-1, keepdims=True)
     gin_ref[...] = (
@@ -348,17 +374,9 @@
     for o in range(1, n):
         sum_copy(o).start()
 
-    acc = ps_send[my_dp].astype(f32)
-    for o in range(1, ndp):
-        ps_copy(o).wait()
-        acc = acc + ps_recv[o].astype(f32)
-    gproj_ref[...] = acc
+    gproj_ref[...] = reduce_last(0)
     for h in range(hh):
-        acc = rs_send[h, my_dp].astype(f32)
-        for o in range(1, ndp):
-            rs_copy(h, o).wait()
-            acc = acc + rs_recv[h, o].astype(f32)
-        gqkv_ref[h] = acc
+        gqkv_ref[h] = reduce_last(1 + h)
 
     for o in range(1, n):
         sum_copy(o).wait()
@@ -428,7 +446,7 @@
         compiler_params=pltpu.CompilerParams(
             collective_id=0, has_side_effects=True, vmem_limit_bytes=63 * 1024 * 1024),
     )(
-        survive, inputs[0], cotangent[0], ln_gain[None], ln_bias[None], qv_bias, proj_bias[None],
+        survive, inputs[0], cotangent[0], ln_gain, ln_bias, qv_bias, proj_bias,
         w_qkv, w_proj,
     )
     grad_w_qkv = gqkv[:, :3 * hw].reshape(hh, 3, hw, rows).transpose(3, 1, 0, 2).reshape(rows, 3, hh * hw)

time: 113 us -> 102 us (0.903)
  Pallas kernels: 98.3 us -> 91.5 us
  local copies, waits for them, and re-layouts: 13 us -> 9.17 us
    pallas_call x1, Pallas kernels: 98.3 us -> 91.5 us  [local(): pl.pallas_call(functools.partial(kernel, n, ndp, hh, hw, grad_scale), out...]
    broadcast_in_dim x3 -> x0, local copies, waits for them, and re-layouts: 3.88 us -> none  [the longest x1 1.29 us: local(): ln_gain[None]]
where the time goes in v2:
time: 102 us
  Pallas kernels  91.5 us (90%)
  local copies, waits for them, and re-layouts  9.17 us (9%)
  between operations  1.3 us (1%)
    pallas_call x1, Pallas kernels, local(): pl.pallas_call(functools.partial(kernel, n, ndp, hh, hw, grad_scale), out...  91.5 us
    unnamed x3, local copies, waits for them, and re-layouts  5.16 us

profile of v2, /device:TPU:0, one launch (start us, length us, event | category | flops | bytes accessed | tf_op | source)
XLA Modules:
  0.0 101.9 jit_solution(3911916853329422998)
XLA Ops:
  1.3 91.5 %shard_map.152 = (bf16[128,1408]{1,0:T(8,128)(2,1)}, bf16[128,1408]{1,0:T(8,128)(2,1)}, f32[176,352]{1,0:T(8,128)}, f32[2,272,352]{2,1,0:T(8,128)}, f32[8,352]{1,0:T(8,128)}) custom-call(f32[1,1]{1,0:T(1,128)} %bitcast.survive_ref, bf16[128,1408]{1,0:T(8,128)(2,1)} %bitcast.19, bf16[128,1408]{1,0:T(8,128)(2,1)} %bitcast.20, f32[1408]{0:T(1024)} %gain_ref.1, ...), custom_call_target="tpu_custom_call" | custom-call | tf_op jit(solution)/shard_map/pallas_call | solution.py:403
  92.7 0.8 constant_dynamic-slice_fusion
  93.5 0.6 slice.18
  94.1 0.5 slice_bitcast_fusion
  94.6 1.2 %slice.15 = f32[2,264,352]{2,1,0:T(8,128)S(1)} slice(f32[2,272,352]{2,1,0:T(8,128)} %get-tuple-element.15), slice={[0:2], [0:264], [0:352]} | slice | bytes 1486848 | tf_op jit(solution)/shard_map/slice | solution.py:452
  95.8 0.9 copy.17
  96.8 1.7 %copy.22 = bf16[1,128,1408]{2,1,0:T(8,128)(2,1)} copy(bf16[1,128,1408]{2,1,0:T(8,128)(2,1)} %bitcast.18) | data formatting | bytes 720896
  98.5 1.7 %copy.23 = bf16[1,128,1408]{2,1,0:T(8,128)(2,1)} copy(bf16[1,128,1408]{2,1,0:T(8,128)(2,1)} %bitcast.17) | data formatting | bytes 720896
  100.2 1.7 %copy.24 = f32[176,352]{1,0:T(8,128)} copy(f32[176,352]{1,0:T(8,128)} %get-tuple-element.32) | data formatting | bytes 495616
